TPU v7x, 768 devices: a whole 4x8x12 slice. The times are simulated.
768 devices in a mesh: blk: 48 (over x, z_lo, core), narrow: 16 (over y, z_hi).
Axes of the slice: x: 4, y: 8, z: 12 (z_hi: 2, z_lo: 6; z = z_hi * 6 + z_lo), core: 2. Of those that a mesh axis runs over, the one named last changes fastest.
Arguments:
- picture_vectors: bfloat16 [196608, 1152], P(('blk', 'narrow')), may hold values from -0.1875 to 0.1875
- caption_vectors: bfloat16 [196608, 1152], P('blk', 'narrow'), may hold values from -0.1875 to 0.1875
- sharpness_weight: float32 [1], replicated, may hold values from 4 to 16
- score_offset_term: float32 [1], replicated, may hold values from -5 to -1
Outputs:
- pair_loss: float32 [196608], P(('blk', 'narrow'))
- image_grad: float32 [196608, 1152], P(('blk', 'narrow'))
- text_grad: float32 [196608, 1152], P('blk', 'narrow')
All inputs are finite; a program needn't handle non-finite values.
Results may differ from a plain program's by a relative error of at most 0.0039.
Values may be sent and summed in bfloat16 or wider, within the bound.
A program may use at most 32 MiB of HBM per device.

v0:
```python
import jax
import jax.numpy as jnp
from jax import lax
from jax.sharding import PartitionSpec as P

EPS = 1e-06


def from_behind(array, axis, by):
    length = lax.axis_size(axis)
    return lax.ppermute(array, axis, [(i, (i + by) % length) for i in range(length)])


def unit_rows(values):
    full = values.astype(jnp.float32)
    norms = jnp.sqrt(jnp.sum(full * full, axis=-1, keepdims=True) + EPS)
    return (full / norms, norms)


def returned_rows(units, norms, direction_derivative):
    inner = jnp.sum(units * direction_derivative, axis=-1, keepdims=True)
    return (direction_derivative - units * inner) / norms


def sign_matrix_tile(left, right, sharpness_factor, offset, positive):
    pair_logits = (
        sharpness_factor * jnp.dot(left, right.T, preferred_element_type=jnp.float32) + offset
    )
    terms = jnp.sum(jax.nn.softplus((1.0 - 2.0 * positive) * pair_logits), axis=-1)
    coef = (sharpness_factor * (jax.nn.sigmoid(pair_logits) - positive)).astype(jnp.bfloat16)
    return (terms, coef)


def left_product(coef, rows):
    return lax.dot_general(coef, rows, (((0,), (0,)), ((), ())), preferred_element_type=jnp.float32)


def per_device(picture_vectors, caption_vectors, sharpness_weight, score_offset_term):
    own_text = lax.all_to_all(caption_vectors, "narrow", split_axis=0, concat_axis=1, tiled=True)
    image_unit, image_norm = unit_rows(picture_vectors)
    unit_text_embed, text_norm = unit_rows(own_text)
    image_low = image_unit.astype(jnp.bfloat16)
    text_low = unit_text_embed.astype(jnp.bfloat16)
    sharpness_factor = sharpness_weight[0]
    offset = score_offset_term[0]
    count = picture_vectors.shape[0]
    ident = jnp.eye(count, dtype=jnp.float32)
    blank = jnp.zeros_like(ident)
    text_below = from_behind(text_low, "blk", 1)
    text_above = from_behind(text_low, "blk", -1)
    loss_own, coef_own = sign_matrix_tile(image_low, text_low, sharpness_factor, offset, ident)
    loss_low, sign_matrix_lesser = sign_matrix_tile(
        image_low, text_below, sharpness_factor, offset, blank
    )
    loss_high, coef_high = sign_matrix_tile(image_low, text_above, sharpness_factor, offset, blank)
    pair_loss = loss_own + loss_low + loss_high
    image_acc = jnp.dot(coef_own, text_low, preferred_element_type=jnp.float32)
    image_acc = image_acc + jnp.dot(
        sign_matrix_lesser, text_below, preferred_element_type=jnp.float32
    )
    image_acc = image_acc + jnp.dot(coef_high, text_above, preferred_element_type=jnp.float32)
    text_acc = left_product(coef_own, image_low)
    part_low = left_product(sign_matrix_lesser, image_low)
    upper_portion = left_product(coef_high, image_low)
    from_above = from_behind(part_low, "blk", -1)
    from_below = from_behind(upper_portion, "blk", 1)
    text_acc = text_acc + from_above + from_below
    image_grad = returned_rows(image_unit, image_norm, image_acc)
    text_full = returned_rows(unit_text_embed, text_norm, text_acc)
    text_grad = lax.all_to_all(text_full, "narrow", split_axis=1, concat_axis=0, tiled=True)
    return (pair_loss, image_grad, text_grad)


def solution(mesh):
    return jax.shard_map(
        per_device,
        mesh=mesh,
        in_specs=(P(("blk", "narrow"), None), P("blk", "narrow"), P(), P()),
        out_specs=(P(("blk", "narrow")), P(("blk", "narrow"), None), P("blk", "narrow")),
        check_vma=False,
    )
```

profile of v0, /device:TPU:280, one launch (start us, length us, event | category | flops | bytes accessed | tf_op | source)
XLA Modules:
  0.0 179.1 jit_solution(8226306893889463859)
XLA Ops:
  0.6 1.1 copy.22
  1.7 48.4 %all_to_all.32 = bf16[16,256,72]{1,2,0:T(8,128)(2,1)S(1)} all-to-all(bf16[16,256,72]{1,2,0:T(8,128)(2,1)S(1)} %bitcast.33), channel_id=1, replica_groups=mesh['blk'=48,'narrow'=16] {'narrow'}, dimensions={0} | all-to-all | bytes 1179648 | tf_op jit(solution)/shard_map/all_to_all | solution.py:39
  50.9 1.9 %collective-permute-start.1 = (bf16[256,1152]{1,0:T(8,128)(2,1)S(1)}, bf16[256,1152]{1,0:T(8,128)(2,1)S(1)}, u32[]{:S(2)}, u32[]{:S(2)}) collective-permute-start(bf16[256,1152]{1,0:T(8,128)(2,1)S(1)} %fusion.12), channel_id=1, source_target_pairs={{0,752},{16,0},{32,16},{48,32},{64,48},{80,64},{96,80},{112,96},{1... | collective-permute-start | bytes 1769480 | tf_op jit(solution)/shard_map/ppermute | solution.py:11
  53.1 2.4 %collective-permute-start = (bf16[256,1152]{1,0:T(8,128)(2,1)S(1)}, bf16[256,1152]{1,0:T(8,128)(2,1)S(1)}, u32[]{:S(2)}, u32[]{:S(2)}) collective-permute-start(bf16[256,1152]{1,0:T(8,128)(2,1)S(1)} %fusion.12), channel_id=1, source_target_pairs={{0,16},{16,32},{32,48},{48,64},{64,80},{80,96},{96,112},{112,128},... | collective-permute-start | bytes 1769480 | tf_op jit(solution)/shard_map/ppermute | solution.py:11
  56.8 10.1 %collective-permute-done.1 = bf16[256,1152]{1,0:T(8,128)(2,1)S(1)} collective-permute-done((bf16[256,1152]{1,0:T(8,128)(2,1)S(1)}, bf16[256,1152]{1,0:T(8,128)(2,1)S(1)}, u32[]{:S(2)}, u32[]{:S(2)}) %collective-permute-start.1) | collective-permute-done | bytes 589856 | tf_op jit(solution)/shard_map/ppermute | solution.py:11
  66.9 0.6 fusion.7
  67.7 0.4 fusion.9
  68.4 2.8 %collective-permute-start.3 = (f32[256,1152]{1,0:T(8,128)S(1)}, f32[256,1152]{1,0:T(8,128)S(1)}, u32[]{:S(2)}, u32[]{:S(2)}) collective-permute-start(f32[256,1152]{1,0:T(8,128)S(1)} %fusion.9), channel_id=1, source_target_pairs={{0,16},{16,32},{32,48},{48,64},{64,80},{80,96},{96,112},{112,128},... | collective-permute-start | bytes 3538952 | tf_op jit(solution)/shard_map/ppermute | solution.py:11
  71.2 0.6 fusion.6
  72.0 0.4 fusion.8
  72.7 4.6 %collective-permute-start.2 = (f32[256,1152]{1,0:T(8,128)S(1)}, f32[256,1152]{1,0:T(8,128)S(1)}, u32[]{:S(2)}, u32[]{:S(2)}) collective-permute-start(f32[256,1152]{1,0:T(8,128)S(1)} %fusion.8), channel_id=1, source_target_pairs={{0,752},{16,0},{32,16},{48,32},{64,48},{80,64},{96,80},{112,96},{1... | collective-permute-start | bytes 3538952 | tf_op jit(solution)/shard_map/ppermute | solution.py:11
  77.3 0.6 fusion.5
  77.9 22.4 %collective-permute-done.3 = f32[256,1152]{1,0:T(8,128)S(1)} collective-permute-done((f32[256,1152]{1,0:T(8,128)S(1)}, f32[256,1152]{1,0:T(8,128)S(1)}, u32[]{:S(2)}, u32[]{:S(2)}) %collective-permute-start.3) | collective-permute-done | bytes 1179680 | tf_op jit(solution)/shard_map/ppermute | solution.py:11
  100.4 0.6 multiply_reduce_fusion
  101.3 1.4 copy.17
  102.7 5.6 %all-to-all-start.1 = ((f32[256,16,72]{0,2,1:T(8,128)}), f32[256,16,72]{0,2,1:T(8,128)S(1)}, u32[]{:S(2)}, u32[]{:S(2)}) async-start(f32[256,16,72]{0,2,1:T(8,128)} %bitcast.4), calls=%async_computation.1 | async-start | bytes 2359296 | tf_op jit(solution)/shard_map/all_to_all | solution.py:70
  108.3 0.4 fusion.10
  108.7 0.6 add_add_fusion
  109.4 0.4 convolution_add_fusion.2
  109.8 0.7 copy-done.8
  110.5 0.5 multiply_reduce_fusion.1
  111.0 1.3 subtract_divide_fusion.1
  112.3 65.6 %all-to-all-done.1 = f32[256,16,72]{0,2,1:T(8,128)S(1)} async-done(((f32[256,16,72]{0,2,1:T(8,128)}), f32[256,16,72]{0,2,1:T(8,128)S(1)}, u32[]{:S(2)}, u32[]{:S(2)}) %all-to-all-start.1) | async-done | bytes 1179680 | tf_op jit(solution)/shard_map/all_to_all | solution.py:70
  178.0 1.1 copy.20
  (31 shorter events, 2.4 us)
Async XLA Ops:
  50.6 2.3 %copy-start = (bf16[256,1152]{1,0:T(8,128)(2,1)S(1)}, bf16[256,1152]{1,0:T(8,128)(2,1)}, u32[]{:S(2)}) copy-start(bf16[256,1152]{1,0:T(8,128)(2,1)} %param.4) | copy-start | bytes 1769476
  50.9 15.9 %collective-permute-start.1 = (bf16[256,1152]{1,0:T(8,128)(2,1)S(1)}, bf16[256,1152]{1,0:T(8,128)(2,1)S(1)}, u32[]{:S(2)}, u32[]{:S(2)}) collective-permute-start(bf16[256,1152]{1,0:T(8,128)(2,1)S(1)} %fusion.12), channel_id=1, source_target_pairs={{0,752},{16,0},{32,16},{48,32},{64,48},{80,64},{96,80},{112,96},{1... | collective-permute-start | bytes 1769480 | tf_op jit(solution)/shard_map/ppermute | solution.py:11
  53.1 18.1 %collective-permute-start = (bf16[256,1152]{1,0:T(8,128)(2,1)S(1)}, bf16[256,1152]{1,0:T(8,128)(2,1)S(1)}, u32[]{:S(2)}, u32[]{:S(2)}) collective-permute-start(bf16[256,1152]{1,0:T(8,128)(2,1)S(1)} %fusion.12), channel_id=1, source_target_pairs={{0,16},{16,32},{32,48},{48,64},{64,80},{80,96},{96,112},{112,128},... | collective-permute-start | bytes 1769480 | tf_op jit(solution)/shard_map/ppermute | solution.py:11
  66.9 0.8 copy-start.7
  67.7 0.7 copy-start.9
  68.4 32.0 %collective-permute-start.3 = (f32[256,1152]{1,0:T(8,128)S(1)}, f32[256,1152]{1,0:T(8,128)S(1)}, u32[]{:S(2)}, u32[]{:S(2)}) collective-permute-start(f32[256,1152]{1,0:T(8,128)S(1)} %fusion.9), channel_id=1, source_target_pairs={{0,16},{16,32},{32,48},{48,64},{64,80},{80,96},{96,112},{112,128},... | collective-permute-start | bytes 3538952 | tf_op jit(solution)/shard_map/ppermute | solution.py:11
  71.2 0.8 copy-start.1
  72.0 0.7 copy-start.5
  72.7 27.7 %collective-permute-start.2 = (f32[256,1152]{1,0:T(8,128)S(1)}, f32[256,1152]{1,0:T(8,128)S(1)}, u32[]{:S(2)}, u32[]{:S(2)}) collective-permute-start(f32[256,1152]{1,0:T(8,128)S(1)} %fusion.8), channel_id=1, source_target_pairs={{0,752},{16,0},{32,16},{48,32},{64,48},{80,64},{96,80},{112,96},{1... | collective-permute-start | bytes 3538952 | tf_op jit(solution)/shard_map/ppermute | solution.py:11
  77.9 23.1 %copy-start.3 = (f32[256,256]{0,1:T(8,128)}, f32[256,256]{0,1:T(8,128)S(1)}, u32[]{:S(2)}) copy-start(f32[256,256]{0,1:T(8,128)S(1)} %get-tuple-element.6) | copy-start | bytes 786436
  102.7 5.6 %copy-start.4 = (f32[256,256]{0,1:T(8,128)S(1)}, f32[256,256]{0,1:T(8,128)}, u32[]{:S(2)}) copy-start(f32[256,256]{0,1:T(8,128)} %copy-done.3) | copy-start | bytes 786436
  102.7 75.3 %all-to-all-start.1 = ((f32[256,16,72]{0,2,1:T(8,128)}), f32[256,16,72]{0,2,1:T(8,128)S(1)}, u32[]{:S(2)}, u32[]{:S(2)}) async-start(f32[256,16,72]{0,2,1:T(8,128)} %bitcast.4), calls=%async_computation.1 | async-start | bytes 2359296 | tf_op jit(solution)/shard_map/all_to_all | solution.py:70
  108.3 1.1 copy-start.2
  108.3 1.1 copy-start.6
  109.4 1.1 copy-start.8
  109.4 1.1 copy-start.10
where the time goes:
time: 180 us; the launch traced here: 179 us
  waiting for transfers between devices  98.2 us (55%)
  blocking collectives  48.4 us (27%)
  starting transfers between devices  17.3 us (10%)
  local copies, waits for them, and re-layouts  5.76 us (3%)
  matrix products  4.63 us (3%)
  other arithmetic  2.76 us (2%)
  between operations  2.11 us (1%)
    all_to_all x1, waiting for transfers between devices, per_device(): lax.all_to_all(text_full, 'narrow', split_axis=1, concat_axis=0, tiled=True)  65.6 us
    all_to_all x1, blocking collectives, per_device(): lax.all_to_all(caption_vectors, 'narrow', split_axis=0, concat_axis=1, ti...  48.4 us
    ppermute x4, waiting for transfers between devices, from_behind(): lax.ppermute(array, axis, [(i, (i + by) % length) for i in range(length)])  32.5 us
    ppermute x4, starting transfers between devices, from_behind(): lax.ppermute(array, axis, [(i, (i + by) % length) for i in range(length)])  11.7 us
    all_to_all x1, starting transfers between devices, per_device(): lax.all_to_all(text_full, 'narrow', split_axis=1, concat_axis=0, tiled=True)  5.6 us
  transfers between devices with their start and end apart: 5, of which 3 were waited for; matrix products, arithmetic and copies ran while one was open for 3% of the time, Pallas kernels for 0%

commit v1 on v0

v1 whole, which is shorter than its diff:
```python
import functools

import jax
import jax.numpy as jnp
from jax import lax
from jax.experimental import pallas as pl
from jax.experimental.pallas import tpu as pltpu
from jax.sharding import PartitionSpec as P

EPS = 1e-06
MESH = pl.DeviceIdType.MESH
F32, BF16 = jnp.float32, jnp.bfloat16


def fold(chunk):
    half = chunk.shape[1] // 2
    return jnp.concatenate([chunk[:, :half], chunk[:, half:]], axis=0)


def unfold(chunk):
    cols = chunk.shape[0] // 2
    return jnp.concatenate([chunk[:cols], chunk[cols:]], axis=1)


def dot(left, right, contract):
    return lax.dot_general(left, right, ((contract[:1], contract[1:]), ((), ())), preferred_element_type=F32)


def softplus(x):
    return jnp.maximum(x, 0.0) + jnp.log1p(jnp.exp(-jnp.abs(x)))


def kernel(
    n_blk, n_narrow,
    pic_ref, cap_ref, sharp_ref, offset_ref,
    loss_ref, image_grad_ref, text_grad_ref,
    image_low, image_turned, packed, got, raw, text_low, back_out, back_in,
    pack_sent, pack_got, image_sent, image_got, text_sent, text_got, back_sent, back_got,
):
    b, n = lax.axis_index("blk"), lax.axis_index("narrow")
    rows, depth = pic_ref.shape
    cols = depth // n_narrow
    above, below = lax.rem(b + 1, n_blk), lax.rem(b + n_blk - 1, n_blk)
    far = 1 - lax.rem(n, 2)

    def peer(k):
        side = jnp.where(k < n_narrow // 2, far, 1 - far)
        step = lax.rem(k + 1, n_narrow // 2)
        return lax.rem(n // 2 + step, n_narrow // 2) * 2 + side

    barrier = pltpu.get_barrier_semaphore()

    def greet(k, carry):
        pl.semaphore_signal(barrier, inc=1, device_id=(b, peer(k)), device_id_type=MESH)
        return carry

    lax.fori_loop(0, n_narrow - 1, greet, 0)
    for other in (above, below):
        pl.semaphore_signal(barrier, inc=1, device_id=(other, n), device_id_type=MESH)

    picture = pic_ref[...].astype(F32)
    image_norm = jnp.sqrt(jnp.sum(picture * picture, axis=1, keepdims=True) + EPS)
    image_low[0] = (picture / image_norm).astype(BF16)

    spot = lambda axis: lax.broadcasted_iota(jnp.int32, (cols, cols), axis)
    turn = (spot(0) == spot(1)).astype(F32).astype(BF16)

    def pack(k, carry):
        block = cap_ref[pl.ds(pl.multiple_of(k * rows, rows), rows), :]
        packed[k] = fold(dot(turn, block, (1, 1))).astype(BF16)
        return carry

    lax.fori_loop(0, n_narrow, pack, 0)
    got[n] = packed[n]

    pl.semaphore_wait(barrier, n_narrow + 1)

    def block_copy(source, target, sent, received, p, here):
        return pltpu.make_async_remote_copy(
            src_ref=source.at[p], dst_ref=target.at[here], send_sem=sent.at[p], recv_sem=received.at[here],
            device_id=(b, p), device_id_type=MESH)

    def whole_copy(buffer, sent, received, slot, other):
        return pltpu.make_async_remote_copy(
            src_ref=buffer.at[0], dst_ref=buffer.at[slot], send_sem=sent.at[slot - 1], recv_sem=received.at[slot - 1],
            device_id=(other, n), device_id_type=MESH)

    def send_packed(k, carry):
        p = peer(k)
        block_copy(packed, got, pack_sent, pack_got, p, n).start()
        return carry

    lax.fori_loop(0, n_narrow // 2, send_packed, 0)
    image_up = whole_copy(image_low, image_sent, image_got, 1, above)
    image_down = whole_copy(image_low, image_sent, image_got, 2, below)
    image_up.start()
    image_down.start()
    lax.fori_loop(n_narrow // 2, n_narrow - 1, send_packed, 0)

    image_turned[:, :rows] = image_low[0].T

    for slot, copy in ((1, image_up), (2, image_down)):
        copy.wait_recv()
        image_turned[:, slot * rows:(slot + 1) * rows] = image_low[slot].T

    def take_packed(k, carry):
        p = peer(k)

        @pl.when(k < n_narrow - 1)
        def _():
            block_copy(packed, got, pack_sent, pack_got, p, p).wait_recv()

        raw[pl.ds(pl.multiple_of(p * cols, 8), cols), :] = unfold(got[p].astype(F32))
        return carry

    lax.fori_loop(0, n_narrow, take_packed, 0)

    text = raw[...]
    text_norm = jnp.sqrt(jnp.sum(text * text, axis=0, keepdims=True) + EPS)
    text_low[0] = (text / text_norm).astype(BF16)
    text_up = whole_copy(text_low, text_sent, text_got, 1, above)
    text_down = whole_copy(text_low, text_sent, text_got, 2, below)
    text_up.start()
    text_down.start()

    sharp, offset = sharp_ref[0], offset_ref[0]
    place = lambda axis: lax.broadcasted_iota(jnp.int32, (rows, rows), axis)
    same = (place(0) == place(1)).astype(F32)

    def tile(image, words):
        return sharp * dot(image, words, (1, 0)) + offset

    def coefs(logits):
        return (sharp * jax.nn.sigmoid(logits)).astype(BF16)

    own_logits = tile(image_low[0], text_low[0])
    own_coef = (sharp * (jax.nn.sigmoid(own_logits) - same)).astype(BF16)
    all_coef = jnp.concatenate(
        [own_coef] + [coefs(tile(image_low[s], text_low[0])) for s in (1, 2)], axis=0)
    text_sum = dot(image_turned[...], all_coef, (1, 0))
    unit = raw[...] / text_norm
    inner = jnp.sum(unit * text_sum, axis=0, keepdims=True)
    text_back = (text_sum - unit * inner) / text_norm
    for p in range(n_narrow):
        back_out[p] = fold(text_back[p * cols:(p + 1) * cols]).astype(BF16)
    back_in[n] = back_out[n]

    def send_back(k, carry):
        block_copy(back_out, back_in, back_sent, back_got, peer(k), n).start()
        return carry

    lax.fori_loop(0, n_narrow - 1, send_back, 0)

    losses = softplus((1.0 - 2.0 * same) * own_logits)
    image_sum = dot(own_coef, text_low[0], (1, 1))
    for slot, copy in ((1, text_up), (2, text_down)):
        copy.wait_recv()
        logits = tile(image_low[0], text_low[slot])
        losses = losses + softplus(logits)
        image_sum = image_sum + dot(coefs(logits), text_low[slot], (1, 1))
    loss_ref[...] = jnp.sum(losses.T, axis=0, keepdims=True)
    picture = pic_ref[...].astype(F32)
    image_unit = picture / image_norm
    image_inner = jnp.sum(image_unit * image_sum, axis=1, keepdims=True)
    image_grad_ref[...] = (image_sum - image_unit * image_inner) / image_norm

    half = rows // 2

    def take_back(k, carry):
        p = peer(k)

        @pl.when(k < n_narrow - 1)
        def _():
            block_copy(back_out, back_in, back_sent, back_got, p, p).wait_recv()

        block = back_in[p].astype(F32)
        for part in range(2):
            text_grad_ref[pl.ds(pl.multiple_of(p * rows + part * half, half), half), :] = (
                block[part * cols:(part + 1) * cols].T)
        return carry

    lax.fori_loop(0, n_narrow, take_back, 0)

    def sent_all(k, carry):
        p = peer(k)
        block_copy(packed, got, pack_sent, pack_got, p, n).wait_send()
        block_copy(back_out, back_in, back_sent, back_got, p, n).wait_send()
        return carry

    lax.fori_loop(0, n_narrow - 1, sent_all, 0)
    for copy in (image_up, image_down, text_up, text_down):
        copy.wait_send()


def solution(mesh):
    n_blk, n_narrow = mesh.shape["blk"], mesh.shape["narrow"]

    def step(pictures, captions, sharpness, offset):
        rows, depth = pictures.shape
        cols = captions.shape[1]
        vmem, smem = pl.BlockSpec(memory_space=pltpu.VMEM), pl.BlockSpec(memory_space=pltpu.SMEM)
        blocks = pltpu.VMEM((n_narrow, 2 * cols, rows // 2), BF16)
        loss, image_grad, text_grad = pl.pallas_call(
            functools.partial(kernel, n_blk, n_narrow),
            out_shape=(
                jax.ShapeDtypeStruct((1, rows), F32),
                jax.ShapeDtypeStruct((rows, depth), F32),
                jax.ShapeDtypeStruct(captions.shape, F32),
            ),
            in_specs=[vmem, vmem, smem, smem],
            out_specs=(vmem, vmem, vmem),
            scratch_shapes=[
                pltpu.VMEM((3, rows, depth), BF16),
                pltpu.VMEM((depth, 3 * rows), BF16),
                blocks,
                blocks,
                pltpu.VMEM((depth, rows), F32),
                pltpu.VMEM((3, depth, rows), BF16),
                blocks,
                blocks,
                pltpu.SemaphoreType.DMA((n_narrow,)),
                pltpu.SemaphoreType.DMA((n_narrow,)),
                pltpu.SemaphoreType.DMA((2,)),
                pltpu.SemaphoreType.DMA((2,)),
                pltpu.SemaphoreType.DMA((2,)),
                pltpu.SemaphoreType.DMA((2,)),
                pltpu.SemaphoreType.DMA((n_narrow,)),
                pltpu.SemaphoreType.DMA((n_narrow,)),
            ],
            compiler_params=pltpu.CompilerParams(
                collective_id=0, has_side_effects=True, vmem_limit_bytes=48 * 2**20),
        )(pictures, captions, sharpness, offset)
        return loss.reshape(rows), image_grad, text_grad

    return jax.shard_map(
        step,
        mesh=mesh,
        in_specs=(P(("blk", "narrow"), None), P("blk", "narrow"), P(), P()),
        out_specs=(P(("blk", "narrow")), P(("blk", "narrow"), None), P("blk", "narrow")),
        check_vma=False,
    )
```

time: 180 us -> 98 us (0.54)
  the two profiles are of different devices: /device:TPU:280 before, /device:TPU:16 now
where the time goes in v1:
time: 98 us; the launch traced here: 97.7 us
  Pallas kernels  88.9 us (91%)
  local copies, waits for them, and re-layouts  6.81 us (7%)
  between operations  1.96 us (2%)
    pallas_call x1, Pallas kernels, step(): pl.pallas_call(functools.partial(kernel, n_blk, n_narrow), out_shape=(jax...  88.9 us
    unnamed x10, local copies, waits for them, and re-layouts  6.81 us

profile of v1, /device:TPU:16, one launch (start us, length us, event | category | flops | bytes accessed | tf_op | source)
XLA Modules:
  0.0 97.7 jit_solution(10645154122730486293)
XLA Ops:
  1.9 1.5 %copy.7.cap_ref = bf16[4096,72]{1,0:T(8,128)(2,1)S(1)} copy(bf16[4096,72]{0,1:T(8,128)(2,1)} %param.5) | data formatting | bytes 1179648 | tf_op args[1]
  3.5 0.0 copy-start.2
  3.5 1.1 %copy-done.2 = bf16[256,1152]{1,0:T(8,128)(2,1)S(1)} copy-done((bf16[256,1152]{1,0:T(8,128)(2,1)S(1)}, bf16[256,1152]{1,0:T(8,128)(2,1)}, u32[]{:S(2)}) %copy-start.2) | copy-done | bytes 589848
  4.5 88.9 %shard_map.67 = (f32[1,256]{1,0:T(1,128)S(1)}, f32[256,1152]{1,0:T(8,128)S(1)}, f32[4096,72]{1,0:T(8,128)S(1)}) custom-call(bf16[256,1152]{1,0:T(8,128)(2,1)S(1)} %copy-done.2, bf16[4096,72]{1,0:T(8,128)(2,1)S(1)} %copy.7.cap_ref, f32[1]{0:T(128)S(6)} %copy.11.sharp_ref, f32[1]{0:T(128)S(6)} %copy.12.offset_ref), custom_call_target="tpu_custom_call" | custom-call | tf_op jit(solution)/shard_map/pallas_call | solution.py:203
  93.5 0.0 copy-start
  93.5 1.0 %copy-done = f32[256,1152]{1,0:T(8,128)} copy-done((f32[256,1152]{1,0:T(8,128)}, f32[256,1152]{1,0:T(8,128)S(1)}, u32[]{:S(2)}) %copy-start) | copy-done | bytes 1179672
  94.5 0.0 copy-start.1
  94.5 1.6 %copy.8 = f32[4096,72]{0,1:T(8,128)} copy(f32[4096,72]{1,0:T(8,128)S(1)} %get-tuple-element.11) | data formatting | bytes 2359296
  96.1 0.6 copy.13
  96.7 0.0 copy-done.1
  96.7 1.0 %copy.14 = f32[256,1152]{1,0:T(8,128)} copy(f32[256,1152]{1,0:T(8,128)S(1)} %copy-done.1) | data formatting | bytes 2359296
Async XLA Ops:
  3.5 1.1 %copy-start.2 = (bf16[256,1152]{1,0:T(8,128)(2,1)S(1)}, bf16[256,1152]{1,0:T(8,128)(2,1)}, u32[]{:S(2)}) copy-start(bf16[256,1152]{1,0:T(8,128)(2,1)} %pic_ref.1) | copy-start | bytes 1769476
  93.5 1.0 %copy-start = (f32[256,1152]{1,0:T(8,128)}, f32[256,1152]{1,0:T(8,128)S(1)}, u32[]{:S(2)}) copy-start(f32[256,1152]{1,0:T(8,128)S(1)} %get-tuple-element.16) | copy-start | bytes 3538948
  94.5 2.2 %copy-start.1 = (f32[256,1152]{1,0:T(8,128)S(1)}, f32[256,1152]{1,0:T(8,128)}, u32[]{:S(2)}) copy-start(f32[256,1152]{1,0:T(8,128)} %copy-done) | copy-start | bytes 3538948

commit v2 on v1

--- a/solution.py
+++ b/solution.py
@@ -62,12 +62,9 @@
     image_norm = jnp.sqrt(jnp.sum(picture * picture, axis=1, keepdims=True) + EPS)
     image_low[0] = (picture / image_norm).astype(BF16)
 
-    spot = lambda axis: lax.broadcasted_iota(jnp.int32, (cols, cols), axis)
-    turn = (spot(0) == spot(1)).astype(F32).astype(BF16)
-
     def pack(k, carry):
-        block = cap_ref[pl.ds(pl.multiple_of(k * rows, rows), rows), :]
-        packed[k] = fold(dot(turn, block, (1, 1))).astype(BF16)
+        block = cap_ref[:, pl.ds(pl.multiple_of(k * rows, rows), rows)]
+        packed[k] = fold(block.astype(F32)).astype(BF16)
         return carry
 
     lax.fori_loop(0, n_narrow, pack, 0)
@@ -164,8 +161,6 @@
     image_inner = jnp.sum(image_unit * image_sum, axis=1, keepdims=True)
     image_grad_ref[...] = (image_sum - image_unit * image_inner) / image_norm
 
-    half = rows // 2
-
     def take_back(k, carry):
         p = peer(k)
 
@@ -173,10 +168,7 @@
         def _():
             block_copy(back_out, back_in, back_sent, back_got, p, p).wait_recv()
 
-        block = back_in[p].astype(F32)
-        for part in range(2):
-            text_grad_ref[pl.ds(pl.multiple_of(p * rows + part * half, half), half), :] = (
-                block[part * cols:(part + 1) * cols].T)
+        text_grad_ref[:, pl.ds(pl.multiple_of(p * rows, rows), rows)] = unfold(back_in[p].astype(F32))
         return carry
 
     lax.fori_loop(0, n_narrow, take_back, 0)
@@ -205,7 +197,7 @@
             out_shape=(
                 jax.ShapeDtypeStruct((1, rows), F32),
                 jax.ShapeDtypeStruct((rows, depth), F32),
-                jax.ShapeDtypeStruct(captions.shape, F32),
+                jax.ShapeDtypeStruct(captions.shape[::-1], F32),
             ),
             in_specs=[vmem, vmem, smem, smem],
             out_specs=(vmem, vmem, vmem),
@@ -229,8 +221,8 @@
             ],
             compiler_params=pltpu.CompilerParams(
                 collective_id=0, has_side_effects=True, vmem_limit_bytes=48 * 2**20),
-        )(pictures, captions, sharpness, offset)
-        return loss.reshape(rows), image_grad, text_grad
+        )(pictures, captions.T, sharpness, offset)
+        return loss.reshape(rows), image_grad, text_grad.T
 
     return jax.shard_map(
         step,

time: 98 us -> 94.4 us (0.963)
  local copies, waits for them, and re-layouts: 6.81 us -> 4.71 us
  Pallas kernels: 88.9 us -> 87.5 us
    unnamed x10 -> x7, local copies, waits for them, and re-layouts: 6.81 us -> 4.71 us
    pallas_call x1, Pallas kernels: 88.9 us -> 87.5 us  [step(): pl.pallas_call(functools.partial(kernel, n_blk, n_narrow), out_shape=(jax...]
where the time goes in v2:
time: 94.4 us; the launch traced here: 94.1 us
  Pallas kernels  87.5 us (93%)
  local copies, waits for them, and re-layouts  4.71 us (5%)
  between operations  1.94 us (2%)
    pallas_call x1, Pallas kernels, step(): pl.pallas_call(functools.partial(kernel, n_blk, n_narrow), out_shape=(jax...  87.5 us
    unnamed x7, local copies, waits for them, and re-layouts  4.71 us

profile of v2, /device:TPU:16, one launch (start us, length us, event | category | flops | bytes accessed | tf_op | source)
XLA Modules:
  0.0 94.1 jit_solution(4875185963116297997)
XLA Ops:
  1.9 0.0 copy-start
  1.9 1.1 %copy-done = bf16[256,1152]{1,0:T(8,128)(2,1)S(1)} copy-done((bf16[256,1152]{1,0:T(8,128)(2,1)S(1)}, bf16[256,1152]{1,0:T(8,128)(2,1)}, u32[]{:S(2)}) %copy-start) | copy-done | bytes 589848
  3.0 0.0 copy-start.1
  3.0 1.1 %copy-done.1 = bf16[4096,72]{0,1:T(8,128)(2,1)S(1)} copy-done((bf16[4096,72]{0,1:T(8,128)(2,1)S(1)}, bf16[4096,72]{0,1:T(8,128)(2,1)}, u32[]{:S(2)}) %copy-start.1) | copy-done | bytes 589848
  4.1 87.5 %shard_map.67 = (f32[1,256]{1,0:T(1,128)S(1)}, f32[256,1152]{1,0:T(8,128)S(1)}, f32[72,4096]{1,0:T(8,128)S(1)}) custom-call(bf16[256,1152]{1,0:T(8,128)(2,1)S(1)} %copy-done, bf16[72,4096]{1,0:T(8,128)(2,1)S(1)} %bitcast.4, f32[1]{0:T(128)S(6)} %copy.10.sharp_ref, f32[1]{0:T(128)S(6)} %copy.11.offset_ref), custom_call_target="tpu_custom_call" | custom-call | tf_op jit(solution)/shard_map/pallas_call | solution.py:195
  91.5 0.6 copy.12
  92.1 1.0 %copy.13 = f32[256,1152]{1,0:T(8,128)} copy(f32[256,1152]{1,0:T(8,128)S(1)} %get-tuple-element.13) | data formatting | bytes 2359296
  93.1 1.0 %copy.14 = f32[4096,72]{0,1:T(8,128)} copy(f32[4096,72]{0,1:T(8,128)S(1)} %bitcast.3) | data formatting | bytes 2359296
Async XLA Ops:
  1.9 1.1 %copy-start = (bf16[256,1152]{1,0:T(8,128)(2,1)S(1)}, bf16[256,1152]{1,0:T(8,128)(2,1)}, u32[]{:S(2)}) copy-start(bf16[256,1152]{1,0:T(8,128)(2,1)} %pic_ref.1) | copy-start | bytes 1769476
  3.0 1.1 %copy-start.1 = (bf16[4096,72]{0,1:T(8,128)(2,1)S(1)}, bf16[4096,72]{0,1:T(8,128)(2,1)}, u32[]{:S(2)}) copy-start(bf16[4096,72]{0,1:T(8,128)(2,1)} %param.5) | copy-start | bytes 1769476

commit v3 on v2

v3 whole, which is shorter than its diff:
```python
import functools

import jax
import jax.numpy as jnp
from jax import lax
from jax.experimental import pallas as pl
from jax.experimental.pallas import tpu as pltpu
from jax.sharding import PartitionSpec as P

EPS = 1e-06
RUN = 12
MESH = pl.DeviceIdType.MESH
F32, BF16 = jnp.float32, jnp.bfloat16


def fold(chunk):
    half = chunk.shape[1] // 2
    return jnp.concatenate([chunk[:, :half], chunk[:, half:]], axis=0)


def unfold(chunk):
    cols = chunk.shape[0] // 2
    return jnp.concatenate([chunk[:cols], chunk[cols:]], axis=1)


def dot(left, right, contract):
    return lax.dot_general(left, right, ((contract[:1], contract[1:]), ((), ())), preferred_element_type=F32)


def softplus(x):
    return jnp.maximum(x, 0.0) + jnp.log1p(jnp.exp(-jnp.abs(x)))


def kernel(
    n_blk, n_narrow, run,
    pic_hbm, cap_hbm, sharp_ref, offset_ref,
    loss_ref, image_grad_ref, text_grad_ref,
    pic_ref, cap_ref, image_low, image_turned, packed, got, raw, text_low, back_out, back_in,
    edge_got, edge_raw, edge_out, edge_in,
    load_sem, pack_sent, pack_got, image_sent, image_got, text_sent, text_got, back_sent, back_got,
    edge_sent, edge_came, edge_back_sent, edge_back_got,
):
    load_picture = pltpu.make_async_copy(pic_hbm, pic_ref, load_sem.at[0])
    load_captions = pltpu.make_async_copy(cap_hbm, cap_ref, load_sem.at[1])
    load_captions.start()
    load_picture.start()

    b, n = lax.axis_index("blk"), lax.axis_index("narrow")
    rows, depth = pic_ref.shape
    cols = depth // n_narrow
    above, below = lax.rem(b + 1, n_blk), lax.rem(b + n_blk - 1, n_blk)
    top, bottom = lax.rem(b, run) == run - 1, lax.rem(b, run) == 0
    edge = jnp.logical_or(top, bottom)
    across = jnp.where(top, above, below)
    across_slot = jnp.where(top, 2, 1)
    far = 1 - lax.rem(n, 2)

    def peer(k):
        side = jnp.where(k < n_narrow // 2, far, 1 - far)
        step = lax.rem(k + 1, n_narrow // 2)
        return lax.rem(n // 2 + step, n_narrow // 2) * 2 + side

    def each(count, body, first=0):
        def step(k, carry):
            body(k)
            return carry
        lax.fori_loop(first, count, step, 0)

    barrier = pltpu.get_barrier_semaphore()

    def greet(blk, narrow):
        pl.semaphore_signal(barrier, inc=1, device_id=(blk, narrow), device_id_type=MESH)

    each(n_narrow - 1, lambda k: greet(b, peer(k)))

    @pl.when(jnp.logical_not(top))
    def _():
        greet(above, n)

    @pl.when(jnp.logical_not(bottom))
    def _():
        greet(below, n)

    @pl.when(edge)
    def _():
        each(n_narrow, lambda k: greet(across, peer(k)))

    load_captions.wait()

    def pack(k):
        block = cap_ref[:, pl.ds(pl.multiple_of(k * rows, rows), rows)]
        packed[k] = fold(block.astype(F32)).astype(BF16)

    each(n_narrow, pack)
    got[n] = packed[n]

    load_picture.wait()
    picture = pic_ref[...].astype(F32)
    image_norm = jnp.sqrt(jnp.sum(picture * picture, axis=1, keepdims=True) + EPS)
    image_low[0] = (picture / image_norm).astype(BF16)

    @pl.when(edge)
    def _():
        image_low[across_slot] = jnp.zeros((rows, depth), BF16)

    @pl.when(edge)
    def _():
        pl.semaphore_wait(barrier, 2 * n_narrow)

    @pl.when(jnp.logical_not(edge))
    def _():
        pl.semaphore_wait(barrier, n_narrow + 1)

    def block_copy(source, target, sent, received, blk, p, here):
        return pltpu.make_async_remote_copy(
            src_ref=source.at[p], dst_ref=target.at[here], send_sem=sent.at[p], recv_sem=received.at[here],
            device_id=(blk, p), device_id_type=MESH)

    def pack_copy(p, here):
        return block_copy(packed, got, pack_sent, pack_got, b, p, here)

    def edge_copy(p, here):
        return block_copy(packed, edge_got, edge_sent, edge_came, across, p, here)

    def back_copy(p, here):
        return block_copy(back_out, back_in, back_sent, back_got, b, p, here)

    def edge_back_copy(p, here):
        return block_copy(edge_out, edge_in, edge_back_sent, edge_back_got, across, p, here)

    def whole_copy(buffer, sent, received, slot):
        return pltpu.make_async_remote_copy(
            src_ref=buffer.at[0], dst_ref=buffer.at[slot], send_sem=sent.at[slot - 1], recv_sem=received.at[slot - 1],
            device_id=(above if slot == 1 else below, n), device_id_type=MESH)

    def to_neighbours(act):
        @pl.when(jnp.logical_not(top))
        def _():
            act(1)

        @pl.when(jnp.logical_not(bottom))
        def _():
            act(2)

    def from_neighbours(slot, act):
        pl.when(jnp.logical_not(bottom if slot == 1 else top))(act)

    each(n_narrow // 2, lambda k: pack_copy(peer(k), n).start())
    each(n_narrow - 1, lambda k: pack_copy(peer(k), n).start(), n_narrow // 2)
    to_neighbours(lambda slot: whole_copy(image_low, image_sent, image_got, slot).start())

    @pl.when(edge)
    def _():
        each(n_narrow, lambda k: edge_copy(peer(k), n).start())


    image_turned[:, :rows] = image_low[0].T
    for slot in (1, 2):
        from_neighbours(slot, lambda: whole_copy(image_low, image_sent, image_got, slot).wait_recv())
        image_turned[:, slot * rows:(slot + 1) * rows] = image_low[slot].T

    def unpack(source, target, p):
        target[pl.ds(pl.multiple_of(p * cols, 8), cols), :] = unfold(source[p].astype(F32))

    def take_packed(k):
        p = peer(k)
        pack_copy(p, p).wait_recv()
        unpack(got, raw, p)

    unpack(got, raw, n)
    each(n_narrow - 1, take_packed)

    def unit_words(words):
        norm = jnp.sqrt(jnp.sum(words * words, axis=0, keepdims=True) + EPS)
        return words / norm, norm

    def split_out(target, text_sum, words):
        unit, norm = unit_words(words)
        inner = jnp.sum(unit * text_sum, axis=0, keepdims=True)
        grad = (text_sum - unit * inner) / norm
        for p in range(n_narrow):
            target[p] = fold(grad[p * cols:(p + 1) * cols]).astype(BF16)

    text_low[0] = unit_words(raw[...])[0].astype(BF16)
    to_neighbours(lambda slot: whole_copy(text_low, text_sent, text_got, slot).start())

    sharp, offset = sharp_ref[0], offset_ref[0]
    place = lambda axis: lax.broadcasted_iota(jnp.int32, (rows, rows), axis)
    same = (place(0) == place(1)).astype(F32)

    def tile(image, words):
        return sharp * dot(image, words, (1, 0)) + offset

    def coefs(logits):
        return (sharp * jax.nn.sigmoid(logits)).astype(BF16)

    own_logits = tile(image_low[0], text_low[0])
    own_coef = (sharp * (jax.nn.sigmoid(own_logits) - same)).astype(BF16)
    all_coef = jnp.concatenate(
        [own_coef] + [coefs(tile(image_low[s], text_low[0])) for s in (1, 2)], axis=0)
    split_out(back_out, dot(image_turned[...], all_coef, (1, 0)), raw[...])
    back_in[n] = back_out[n]
    each(n_narrow - 1, lambda k: back_copy(peer(k), n).start())

    @pl.when(edge)
    def _():
        def take_across(k):
            p = peer(k)
            edge_copy(p, p).wait_recv()
            unpack(edge_got, edge_raw, p)

        each(n_narrow, take_across)
        words = unit_words(edge_raw[...])[0].astype(BF16)
        text_low[across_slot] = words
        part = dot(image_turned[:, :rows], coefs(tile(image_low[0], words)), (1, 0))
        split_out(edge_out, part, edge_raw[...])
        each(n_narrow, lambda k: edge_back_copy(peer(k), n).start())

    losses = softplus((1.0 - 2.0 * same) * own_logits)
    image_sum = dot(own_coef, text_low[0], (1, 1))
    for slot in (1, 2):
        from_neighbours(slot, lambda: whole_copy(text_low, text_sent, text_got, slot).wait_recv())
        logits = tile(image_low[0], text_low[slot])
        losses = losses + softplus(logits)
        image_sum = image_sum + dot(coefs(logits), text_low[slot], (1, 1))
    loss_ref[...] = jnp.sum(losses.T, axis=0, keepdims=True)
    image_unit = pic_ref[...].astype(F32) / image_norm
    image_inner = jnp.sum(image_unit * image_sum, axis=1, keepdims=True)
    image_grad_ref[...] = (image_sum - image_unit * image_inner) / image_norm

    def block_of(p):
        return (slice(None), pl.ds(pl.multiple_of(p * rows, rows), rows))

    def take_back(k):
        p = peer(k)
        back_copy(p, p).wait_recv()
        text_grad_ref[block_of(p)] = unfold(back_in[p].astype(F32))

    text_grad_ref[block_of(n)] = unfold(back_in[n].astype(F32))
    each(n_narrow - 1, take_back)

    @pl.when(edge)
    def _():
        def take_edge(k):
            p = peer(k)
            edge_back_copy(p, p).wait_recv()
            text_grad_ref[block_of(p)] += unfold(edge_in[p].astype(F32))

        each(n_narrow, take_edge)

    def sent_all(k):
        pack_copy(peer(k), n).wait_send()
        back_copy(peer(k), n).wait_send()

    each(n_narrow - 1, sent_all)

    def sent_whole(slot):
        whole_copy(image_low, image_sent, image_got, slot).wait_send()
        whole_copy(text_low, text_sent, text_got, slot).wait_send()

    to_neighbours(sent_whole)

    @pl.when(edge)
    def _():
        def sent_across(k):
            edge_copy(peer(k), n).wait_send()
            edge_back_copy(peer(k), n).wait_send()

        each(n_narrow, sent_across)


def hand_out(loss, image_grad, text_grad, loss_out, image_out, text_out, sems):
    copies = [
        pltpu.make_async_copy(source, target, sems.at[i])
        for i, (source, target) in enumerate(((text_grad, text_out), (image_grad, image_out), (loss, loss_out)))]
    for copy in copies:
        copy.start()
    for copy in copies:
        copy.wait()


def solution(mesh):
    n_blk, n_narrow = mesh.shape["blk"], mesh.shape["narrow"]

    def step(pictures, captions, sharpness, offset):
        rows, depth = pictures.shape
        words = captions.T
        vmem, smem = pl.BlockSpec(memory_space=pltpu.VMEM), pl.BlockSpec(memory_space=pltpu.SMEM)
        hbm = pl.BlockSpec(memory_space=pltpu.HBM)
        blocks = pltpu.VMEM((n_narrow, 2 * words.shape[0], rows // 2), BF16)
        per_peer, per_side = pltpu.SemaphoreType.DMA((n_narrow,)), pltpu.SemaphoreType.DMA((2,))
        outs = (
            jax.ShapeDtypeStruct((1, rows), F32),
            jax.ShapeDtypeStruct((rows, depth), F32),
            jax.ShapeDtypeStruct(words.shape, F32),
        )
        results = pl.pallas_call(
            functools.partial(kernel, n_blk, n_narrow, RUN),
            out_shape=outs,
            in_specs=[hbm, hbm, smem, smem],
            out_specs=(vmem, vmem, vmem),
            scratch_shapes=[
                pltpu.VMEM(pictures.shape, BF16),
                pltpu.VMEM(words.shape, BF16),
                pltpu.VMEM((3, rows, depth), BF16),
                pltpu.VMEM((depth, 3 * rows), BF16),
                blocks,
                blocks,
                pltpu.VMEM((depth, rows), F32),
                pltpu.VMEM((3, depth, rows), BF16),
                blocks,
                blocks,
                blocks,
                pltpu.VMEM((depth, rows), F32),
                blocks,
                blocks,
                per_side,
                per_peer, per_peer,
                per_side, per_side,
                per_side, per_side,
                per_peer, per_peer,
                per_peer, per_peer,
                per_peer, per_peer,
            ],
            compiler_params=pltpu.CompilerParams(
                collective_id=0, has_side_effects=True, vmem_limit_bytes=48 * 2**20),
        )(*(pltpu.with_memory_space_constraint(x, pltpu.HBM) for x in (pictures, words)), sharpness, offset)
        loss, image_grad, text_grad = pl.pallas_call(
            hand_out,
            out_shape=outs,
            in_specs=[vmem] * 3,
            out_specs=(hbm,) * 3,
            scratch_shapes=[pltpu.SemaphoreType.DMA((3,))],
            compiler_params=pltpu.CompilerParams(vmem_limit_bytes=2**20),
        )(*results)
        return loss.reshape(rows), image_grad, text_grad.T

    return jax.shard_map(
        step,
        mesh=mesh,
        in_specs=(P(("blk", "narrow"), None), P("blk", "narrow"), P(), P()),
        out_specs=(P(("blk", "narrow")), P(("blk", "narrow"), None), P("blk", "narrow")),
        check_vma=False,
    )
```

time: 94.4 us -> 83.8 us (0.89)
  the two profiles are of different devices: /device:TPU:16 before, /device:TPU:66 now
where the time goes in v3:
time: 83.8 us; the launch traced here: 83.7 us
  Pallas kernels  81.7 us (97%)
  between operations  1.93 us (2%)
    pallas_call x1, Pallas kernels, step(): pl.pallas_call(functools.partial(kernel, n_blk, n_narrow, RUN), out_shape...  80.3 us

profile of v3, /device:TPU:66, one launch (start us, length us, event | category | flops | bytes accessed | tf_op | source)
XLA Modules:
  0.0 83.7 jit_solution(14685614708708546258)
XLA Ops:
  1.9 80.3 %shard_map.67 = (f32[1,256]{1,0:T(1,128)S(1)}, f32[256,1152]{1,0:T(8,128)S(1)}, f32[72,4096]{1,0:T(8,128)S(1)}) custom-call(bf16[256,1152]{1,0:T(8,128)(2,1)} %pic_hbm.1, bf16[72,4096]{1,0:T(8,128)(2,1)} %bitcast.3, f32[1]{0:T(128)S(6)} %copy.7.sharp_ref, f32[1]{0:T(128)S(6)} %copy.8.offset_ref), custom_call_target="tpu_custom_call" | custom-call | tf_op jit(solution)/shard_map/pallas_call | solution.py:297
  82.2 1.4 %shard_map.68 = (f32[1,256]{1,0:T(1,128)}, f32[256,1152]{1,0:T(8,128)}, f32[72,4096]{1,0:T(8,128)}) custom-call(f32[1,256]{1,0:T(1,128)S(1)} %get-tuple-element.9.loss, f32[256,1152]{1,0:T(8,128)S(1)} %get-tuple-element.10.image_grad, f32[72,4096]{1,0:T(8,128)S(1)} %get-tuple-element.11.text_grad), custom_call_target="tpu_custom_call" | custom-call | tf_op jit(solution)/shard_map/pallas_call | solution.py:328

commit v4 on v3

--- a/solution.py
+++ b/solution.py
@@ -38,7 +38,7 @@
     pic_ref, cap_ref, image_low, image_turned, packed, got, raw, text_low, back_out, back_in,
     edge_got, edge_raw, edge_out, edge_in,
     load_sem, pack_sent, pack_got, image_sent, image_got, text_sent, text_got, back_sent, back_got,
-    edge_sent, edge_came, edge_back_sent, edge_back_got,
+    edge_sent, edge_came, edge_back_sent, edge_back_got, beside,
 ):
     load_picture = pltpu.make_async_copy(pic_hbm, pic_ref, load_sem.at[0])
     load_captions = pltpu.make_async_copy(cap_hbm, cap_ref, load_sem.at[1])
@@ -60,6 +60,12 @@
         step = lax.rem(k + 1, n_narrow // 2)
         return lax.rem(n // 2 + step, n_narrow // 2) * 2 + side
 
+    half = n_narrow // 2
+    own_side = lax.rem(n, 2) * half
+
+    def spot(p):
+        return lax.rem(p, 2) * half + p // 2
+
     def each(count, body, first=0):
         def step(k, carry):
             body(k)
@@ -92,16 +98,7 @@
         packed[k] = fold(block.astype(F32)).astype(BF16)
 
     each(n_narrow, pack)
-    got[n] = packed[n]
-
-    load_picture.wait()
-    picture = pic_ref[...].astype(F32)
-    image_norm = jnp.sqrt(jnp.sum(picture * picture, axis=1, keepdims=True) + EPS)
-    image_low[0] = (picture / image_norm).astype(BF16)
-
-    @pl.when(edge)
-    def _():
-        image_low[across_slot] = jnp.zeros((rows, depth), BF16)
+    got[spot(n)] = packed[n]
 
     @pl.when(edge)
     def _():
@@ -117,7 +114,9 @@
             device_id=(blk, p), device_id_type=MESH)
 
     def pack_copy(p, here):
-        return block_copy(packed, got, pack_sent, pack_got, b, p, here)
+        return pltpu.make_async_remote_copy(
+            src_ref=packed.at[p], dst_ref=got.at[spot(here)], send_sem=pack_sent.at[p], recv_sem=pack_got.at[here],
+            device_id=(b, p), device_id_type=MESH)
 
     def edge_copy(p, here):
         return block_copy(packed, edge_got, edge_sent, edge_came, across, p, here)
@@ -133,6 +132,13 @@
             src_ref=buffer.at[0], dst_ref=buffer.at[slot], send_sem=sent.at[slot - 1], recv_sem=received.at[slot - 1],
             device_id=(above if slot == 1 else below, n), device_id_type=MESH)
 
+    def text_copy(slot, far_side):
+        part = pl.ds(half - own_side if far_side else own_side, half)
+        sem = 2 * (slot - 1) + far_side
+        return pltpu.make_async_remote_copy(
+            src_ref=got.at[part], dst_ref=beside.at[slot - 1, part], send_sem=text_sent.at[sem], recv_sem=text_got.at[sem],
+            device_id=(above if slot == 1 else below, n), device_id_type=MESH)
+
     def to_neighbours(act):
         @pl.when(jnp.logical_not(top))
         def _():
@@ -147,6 +153,17 @@
 
     each(n_narrow // 2, lambda k: pack_copy(peer(k), n).start())
     each(n_narrow - 1, lambda k: pack_copy(peer(k), n).start(), n_narrow // 2)
+
+    load_picture.wait()
+    picture = pic_ref[...].astype(F32)
+    image_norm = jnp.sqrt(jnp.sum(picture * picture, axis=1, keepdims=True) + EPS)
+    image_scale = 1.0 / image_norm
+    image_low[0] = (picture * image_scale).astype(BF16)
+
+    @pl.when(edge)
+    def _():
+        image_low[across_slot] = jnp.zeros((rows, depth), BF16)
+
     to_neighbours(lambda slot: whole_copy(image_low, image_sent, image_got, slot).start())
 
     @pl.when(edge)
@@ -154,35 +171,38 @@
         each(n_narrow, lambda k: edge_copy(peer(k), n).start())
 
 
+    def unpack(source, target, p, place):
+        target[pl.ds(pl.multiple_of(p * cols, 8), cols), :] = unfold(source[place].astype(F32))
+
+    def take_packed(k):
+        p = peer(k)
+        pack_copy(p, p).wait_recv()
+        unpack(got, raw, p, spot(p))
+
     image_turned[:, :rows] = image_low[0].T
+    unpack(got, raw, n, spot(n))
+    each(n_narrow - 1, take_packed, half)
+    to_neighbours(lambda slot: text_copy(slot, 0).start())
+
     for slot in (1, 2):
         from_neighbours(slot, lambda: whole_copy(image_low, image_sent, image_got, slot).wait_recv())
         image_turned[:, slot * rows:(slot + 1) * rows] = image_low[slot].T
 
-    def unpack(source, target, p):
-        target[pl.ds(pl.multiple_of(p * cols, 8), cols), :] = unfold(source[p].astype(F32))
-
-    def take_packed(k):
-        p = peer(k)
-        pack_copy(p, p).wait_recv()
-        unpack(got, raw, p)
-
-    unpack(got, raw, n)
-    each(n_narrow - 1, take_packed)
+    each(half, take_packed)
+    to_neighbours(lambda slot: text_copy(slot, 1).start())
 
     def unit_words(words):
-        norm = jnp.sqrt(jnp.sum(words * words, axis=0, keepdims=True) + EPS)
-        return words / norm, norm
+        scale = 1.0 / jnp.sqrt(jnp.sum(words * words, axis=0, keepdims=True) + EPS)
+        return words * scale, scale
 
     def split_out(target, text_sum, words):
-        unit, norm = unit_words(words)
+        unit, scale = unit_words(words)
         inner = jnp.sum(unit * text_sum, axis=0, keepdims=True)
-        grad = (text_sum - unit * inner) / norm
+        grad = (text_sum - unit * inner) * scale
         for p in range(n_narrow):
             target[p] = fold(grad[p * cols:(p + 1) * cols]).astype(BF16)
 
     text_low[0] = unit_words(raw[...])[0].astype(BF16)
-    to_neighbours(lambda slot: whole_copy(text_low, text_sent, text_got, slot).start())
 
     sharp, offset = sharp_ref[0], offset_ref[0]
     place = lambda axis: lax.broadcasted_iota(jnp.int32, (rows, rows), axis)
@@ -194,10 +214,10 @@
     def coefs(logits):
         return (sharp * jax.nn.sigmoid(logits)).astype(BF16)
 
-    own_logits = tile(image_low[0], text_low[0])
+    logits = tile(image_low[...].reshape(3 * rows, depth), text_low[0])
+    own_logits = logits[:rows]
     own_coef = (sharp * (jax.nn.sigmoid(own_logits) - same)).astype(BF16)
-    all_coef = jnp.concatenate(
-        [own_coef] + [coefs(tile(image_low[s], text_low[0])) for s in (1, 2)], axis=0)
+    all_coef = jnp.concatenate([own_coef, coefs(logits[rows:])], axis=0)
     split_out(back_out, dot(image_turned[...], all_coef, (1, 0)), raw[...])
     back_in[n] = back_out[n]
     each(n_narrow - 1, lambda k: back_copy(peer(k), n).start())
@@ -207,7 +227,7 @@
         def take_across(k):
             p = peer(k)
             edge_copy(p, p).wait_recv()
-            unpack(edge_got, edge_raw, p)
+            unpack(edge_got, edge_raw, p, p)
 
         each(n_narrow, take_across)
         words = unit_words(edge_raw[...])[0].astype(BF16)
@@ -219,14 +239,20 @@
     losses = softplus((1.0 - 2.0 * same) * own_logits)
     image_sum = dot(own_coef, text_low[0], (1, 1))
     for slot in (1, 2):
-        from_neighbours(slot, lambda: whole_copy(text_low, text_sent, text_got, slot).wait_recv())
+        def take_beside():
+            for side in range(2):
+                text_copy(slot, side).wait_recv()
+            each(n_narrow, lambda p: unpack(beside.at[slot - 1], edge_raw, p, spot(p)))
+            text_low[slot] = unit_words(edge_raw[...])[0].astype(BF16)
+
+        from_neighbours(slot, take_beside)
         logits = tile(image_low[0], text_low[slot])
         losses = losses + softplus(logits)
         image_sum = image_sum + dot(coefs(logits), text_low[slot], (1, 1))
     loss_ref[...] = jnp.sum(losses.T, axis=0, keepdims=True)
-    image_unit = pic_ref[...].astype(F32) / image_norm
+    image_unit = pic_ref[...].astype(F32) * image_scale
     image_inner = jnp.sum(image_unit * image_sum, axis=1, keepdims=True)
-    image_grad_ref[...] = (image_sum - image_unit * image_inner) / image_norm
+    image_grad_ref[...] = (image_sum - image_unit * image_inner) * image_scale
 
     def block_of(p):
         return (slice(None), pl.ds(pl.multiple_of(p * rows, rows), rows))
@@ -256,7 +282,8 @@
 
     def sent_whole(slot):
         whole_copy(image_low, image_sent, image_got, slot).wait_send()
-        whole_copy(text_low, text_sent, text_got, slot).wait_send()
+        for side in range(2):
+            text_copy(slot, side).wait_send()
 
     to_neighbours(sent_whole)
 
@@ -317,10 +344,11 @@
                 per_side,
                 per_peer, per_peer,
                 per_side, per_side,
-                per_side, per_side,
+                pltpu.SemaphoreType.DMA((4,)), pltpu.SemaphoreType.DMA((4,)),
                 per_peer, per_peer,
                 per_peer, per_peer,
                 per_peer, per_peer,
+                pltpu.VMEM((2, n_narrow, 2 * words.shape[0], rows // 2), BF16),
             ],
             compiler_params=pltpu.CompilerParams(
                 collective_id=0, has_side_effects=True, vmem_limit_bytes=48 * 2**20),

time: 83.8 us -> 83.6 us (level)
  the two profiles are of different devices: /device:TPU:66 before, /device:TPU:1 now
where the time goes in v4:
time: 83.6 us; the launch traced here: 83.4 us
  Pallas kernels  81.5 us (97%)
  between operations  1.93 us (2%)
    pallas_call x1, Pallas kernels, step(): pl.pallas_call(functools.partial(kernel, n_blk, n_narrow, RUN), out_shape...  80 us

profile of v4, /device:TPU:1, one launch (start us, length us, event | category | flops | bytes accessed | tf_op | source)
XLA Modules:
  0.0 83.4 jit_solution(12848312335635388248)
XLA Ops:
  1.9 80.0 %shard_map.67 = (f32[1,256]{1,0:T(1,128)S(1)}, f32[256,1152]{1,0:T(8,128)S(1)}, f32[72,4096]{1,0:T(8,128)S(1)}) custom-call(bf16[256,1152]{1,0:T(8,128)(2,1)} %pic_hbm.1, bf16[72,4096]{1,0:T(8,128)(2,1)} %bitcast.3, f32[1]{0:T(128)S(6)} %copy.7.sharp_ref, f32[1]{0:T(128)S(6)} %copy.8.offset_ref), custom_call_target="tpu_custom_call" | custom-call | tf_op jit(solution)/shard_map/pallas_call | solution.py:324
  82.0 1.4 %shard_map.68 = (f32[1,256]{1,0:T(1,128)}, f32[256,1152]{1,0:T(8,128)}, f32[72,4096]{1,0:T(8,128)}) custom-call(f32[1,256]{1,0:T(1,128)S(1)} %get-tuple-element.9.loss, f32[256,1152]{1,0:T(8,128)S(1)} %get-tuple-element.10.image_grad, f32[72,4096]{1,0:T(8,128)S(1)} %get-tuple-element.11.text_grad), custom_call_target="tpu_custom_call" | custom-call | tf_op jit(solution)/shard_map/pallas_call | solution.py:356
